TPU v7x, 32 devices: a whole 2x2x4 slice. The times are simulated.
32 devices in a mesh: lat: 8 (over z, y), lon: 4 (over x, core).
Axes of the slice: x: 2, y: 2, z: 4, core: 2. Of those that a mesh axis runs over, the one named last changes fastest.
Arguments:
- meridian_slab_data: bfloat16 [256, 96, 1024], P('lat', None, 'lon'), may hold values from -6 to 6
- smoothing_filter_taps: bfloat16 [3, 3, 96, 128], replicated, may hold values from -0.21875 to 0.21875
- smoothing_offset_entries: float32 [128], replicated, may hold values from -3 to 3
- opening_coarsen_taps: bfloat16 [4, 4, 128, 256], replicated, may hold values from -0.125 to 0.125
- opening_coarsen_offset: float32 [256], replicated, may hold values from -3 to 3
- closing_coarsen_taps: bfloat16 [4, 4, 256, 256], replicated, may hold values from -0.09375 to 0.09375
- closing_coarsen_offset: float32 [256], replicated, may hold values from -3 to 3
- layernorm_multiplier: float32 [256], replicated, may hold values from 0.25 to 1.75
- triple_mapping_matrix: bfloat16 [256, 768], replicated, may hold values from -0.375 to 0.375
- logit_sharpness: float32 [8], replicated, may hold values from 2.5 to 40, as said below
- mixing_return_matrix: bfloat16 [256, 256], replicated, may hold values from -0.375 to 0.375
Outputs:
- encoded: bfloat16 [64, 256, 256], P('lat', 'lon')
Inputs may be any that keep to these rules, and one draw needn't show every extreme that they name: `logit_sharpness`: per-head score scales.
All inputs are finite; a program needn't handle non-finite values.
Results may differ from a plain program's by a relative error of at most 0.034.
Values may be sent and summed in bfloat16 or wider, within the bound.
A program may use at most 128 MiB of HBM per device.

v0:
```python
import jax
import jax.numpy as jnp
from jax import lax
from jax.sharding import PartitionSpec as P

HEADS = 8


def extended_2(value, sides, width):
    for axis, dim in sides:
        size, length = (lax.axis_size(axis), value.shape[dim])
        up = [(i, (i + 1) % size) for i in range(size)]
        down = [(j, i) for i, j in up]
        last = lax.slice_in_dim(value, length - width, length, axis=dim)
        initial = lax.slice_in_dim(value, 0, width, axis=dim)
        before = lax.ppermute(last, axis, up)
        after = lax.ppermute(initial, axis, down)
        value = jnp.concatenate([before, value, after], axis=dim)
    return value


def clear_edges(extended):
    count = extended.shape[0]
    index = lax.axis_index("lat")
    last = lax.axis_size("lat") - 1
    rows = jnp.arange(count)
    cut = (rows < 1) & (index == 0) | (rows >= count - 1) & (index == last)
    shape = (count,) + (1,) * (extended.ndim - 1)
    return jnp.where(cut.reshape(shape), jnp.zeros_like(extended), extended)


def first_conv(extended, kernel, bias):
    total = lax.conv_general_dilated(
        extended[None],
        kernel,
        (1, 1),
        "VALID",
        dimension_numbers=("NHCW", "HWIO", "NHWC"),
        preferred_element_type=jnp.float32,
    )[0]
    return jax.nn.silu(total + bias).astype(jnp.bfloat16)


def halving_filter(extended, kernel, bias):
    total = lax.conv_general_dilated(
        extended[None],
        kernel,
        (2, 2),
        "VALID",
        dimension_numbers=("NHWC", "HWIO", "NHWC"),
        preferred_element_type=jnp.float32,
    )[0]
    return jax.nn.silu(total + bias).astype(jnp.bfloat16)


def on_device(
    meridian_slab_data,
    smoothing_filter_taps,
    smoothing_offset_entries,
    opening_coarsen_taps,
    opening_coarsen_offset,
    closing_coarsen_taps,
    closing_coarsen_offset,
    layernorm_multiplier,
    triple_mapping_matrix,
    logit_sharpness,
    mixing_return_matrix,
):
    extended = extended_2(meridian_slab_data, (("lat", 0), ("lon", 2)), 1)
    extended = clear_edges(extended)
    opening_halved = first_conv(extended, smoothing_filter_taps, smoothing_offset_entries)
    opening_halved_padded = clear_edges(extended_2(opening_halved, (("lat", 0), ("lon", 1)), 1))
    closing_halved = halving_filter(
        opening_halved_padded, opening_coarsen_taps, opening_coarsen_offset
    )
    closing_halved_padded = clear_edges(extended_2(closing_halved, (("lat", 0), ("lon", 1)), 1))
    activation_maps = halving_filter(
        closing_halved_padded, closing_coarsen_taps, closing_coarsen_offset
    )
    rows, tokens, widths = activation_maps.shape
    per_group_channel_count = widths // HEADS
    upcast = activation_maps.astype(jnp.float32)
    mean = jnp.mean(upcast, axis=-1, keepdims=True)
    centred = upcast - mean
    variance = jnp.mean(centred * centred, axis=-1, keepdims=True)
    normed = (centred * lax.rsqrt(variance + 1e-05) * layernorm_multiplier).astype(jnp.bfloat16)
    projected = jnp.dot(normed, triple_mapping_matrix, preferred_element_type=jnp.float32)
    shape = (rows, tokens, HEADS, per_group_channel_count)
    logit_multiplier = (logit_sharpness / jnp.sqrt(jnp.float32(per_group_channel_count)))[:, None]
    query = (projected[..., :widths].reshape(shape) * logit_multiplier).astype(jnp.bfloat16)
    key = projected[..., widths : 2 * widths].reshape(shape).astype(jnp.bfloat16)
    value = projected[..., 2 * widths :].reshape(shape).astype(jnp.bfloat16)

    def as_items(array):
        return jnp.transpose(array, (0, 2, 1, 3)).reshape(
            rows * HEADS, tokens, per_group_channel_count
        )

    query_items = as_items(query)
    key_items = as_items(key)
    value_items = as_items(value)
    start_best = jnp.full((rows * HEADS, tokens), -1e30, jnp.float32)
    start_sum = jnp.zeros((rows * HEADS, tokens), jnp.float32)
    start_accum = jnp.zeros((rows * HEADS, tokens, per_group_channel_count), jnp.float32)
    best = start_best
    weight_sum = start_sum
    accum = start_accum
    key_part = lax.all_gather(key_items, "lon", axis=1, tiled=True)
    value_part = lax.all_gather(value_items, "lon", axis=1, tiled=True)
    scores = jnp.einsum("itd,isd->its", query_items, key_part, preferred_element_type=jnp.float32)
    new_best = jnp.maximum(best, jnp.max(scores, axis=-1))
    factor = jnp.exp(best - new_best)
    weights = jnp.exp(scores - new_best[..., None])
    weight_sum = weight_sum * factor + jnp.sum(weights, axis=-1)
    accum = accum * factor[..., None] + jnp.einsum(
        "its,isd->itd", weights.astype(jnp.bfloat16), value_part, preferred_element_type=jnp.float32
    )
    best, weight_sum, accum = (new_best, weight_sum, accum)
    attended = (
        (accum / weight_sum[..., None])
        .astype(jnp.bfloat16)
        .reshape(rows, HEADS, tokens, per_group_channel_count)
    )
    joined = jnp.transpose(attended, (0, 2, 1, 3)).reshape(rows, tokens, widths)
    mixed_out = jnp.dot(joined, mixing_return_matrix, preferred_element_type=jnp.float32)
    return (upcast + mixed_out).astype(jnp.bfloat16)


def solution(mesh):
    return jax.shard_map(
        on_device,
        mesh=mesh,
        in_specs=(P("lat", None, "lon"), P(), P(), P(), P(), P(), P(), P(), P(), P(), P()),
        out_specs=P("lat", "lon", None),
        check_vma=False,
    )
```

profile of v0, /device:TPU:17, one launch (start us, length us, event | category | flops | bytes accessed | tf_op | source)
XLA Modules:
  0.0 142.0 jit_solution(15877996708247512220)
XLA Ops:
  6.5 4.6 %copy.42 = bf16[32,96,256]{1,0,2:T(8,128)(2,1)} copy(bf16[32,96,256]{2,1,0:T(8,128)(2,1)} %param.11) | data formatting | bytes 3145728 | tf_op args[0]
  15.0 2.9 %collective-permute-done = bf16[1,96,256]{1,0,2:T(2,128)(2,1)S(1)} collective-permute-done((bf16[1,96,256]{1,0,2:T(2,128)(2,1)S(1)}, bf16[1,96,256]{1,0,2:T(2,128)(2,1)S(1)}, u32[]{:S(2)}, u32[]{:S(2)}) %collective-permute-start) | collective-permute-done | bytes 49184 | tf_op jit(solution)/shard_map/ppermute | solution.py:16
  17.9 3.9 %collective-permute-done.1 = bf16[1,96,256]{1,0,2:T(2,128)(2,1)S(1)} collective-permute-done((bf16[1,96,256]{1,0,2:T(2,128)(2,1)S(1)}, bf16[1,96,256]{1,0,2:T(2,128)(2,1)S(1)}, u32[]{:S(2)}, u32[]{:S(2)}) %collective-permute-start.1) | collective-permute-done | bytes 49184 | tf_op jit(solution)/shard_map/ppermute | solution.py:17
  21.8 3.1 %fusion.80 = (bf16[1,34,96,256]{2,1,3,0:T(8,128)(2,1)S(1)}, bf16[34,96,256]{1,0,2:T(8,128)(2,1)S(1)}) fusion(bf16[1,96,256]{1,0,2:T(2,128)(2,1)S(1)} %collective-permute-done.1, bf16[32,96,256]{1,0,2:T(8,128)(2,1)} %copy.42, bf16[1,96,256]{1,0,2:T(2,128)(2,1)S(1)} %collective-permute-done), kind=kLoop, calls=%fused_computation.91 | loop fusion | flops 5013504 | bytes 5013504 | tf_op jit(solution)/shard_map/concatenate | solution.py:18
  27.3 2.3 %collective-permute-done.3 = bf16[34,96,1]{1,0,2:T(8,128)(2,1)S(1)} collective-permute-done((bf16[34,96,1]{1,0,2:T(8,128)(2,1)S(1)}, bf16[34,96,1]{1,0,2:T(8,128)(2,1)S(1)}, u32[]{:S(2)}, u32[]{:S(2)}) %collective-permute-start.3) | collective-permute-done | bytes 6560 | tf_op jit(solution)/shard_map/ppermute | solution.py:17
  31.8 4.6 %broadcast_select_fusion = f32[32,8,33,128]{3,1,2,0:T(8,128)S(1)} fusion(pred[8,33]{0,1:T(8,128)(4,1)S(1)} %copy-done.11, bf16[3,3,96,128]{3,2,1,0:T(8,128)(2,1)S(1)} %copy-done.9, bf16[34,96,1,7,2]{1,3,4,0,2:T(8,128)(2,1)S(1)} %slice.72, bf16[34,96,1,8,33]{1,3,4,0,2:T(8,128)(2,1)S(1)} %copy.47), kind=kOutput, calls=%fused_computation.30 | convolution fusion | flops 1875127296 | bytes 6361608 | tf_op jit(solution)/shard_map/conv_general_dilated | solution.py:33
  39.0 2.0 %collective-permute-start.5 = (bf16[1,256,128]{2,0,1:T(2,128)(2,1)S(1)}, bf16[1,256,128]{2,0,1:T(2,128)(2,1)S(1)}, u32[]{:S(2)}, u32[]{:S(2)}) collective-permute-start(bf16[1,256,128]{2,0,1:T(2,128)(2,1)S(1)} %get-tuple-element.16), channel_id=1, source_target_pairs={{4,0},{8,4},{12,8},{16,12},{20,16},{24,20},{28,24},{0,28},{5,1},{9... | collective-permute-start | bytes 196616 | tf_op jit(solution)/shard_map/ppermute | solution.py:17
  41.0 3.3 %collective-permute-done.4 = bf16[1,256,128]{2,0,1:T(2,128)(2,1)S(1)} collective-permute-done((bf16[1,256,128]{2,0,1:T(2,128)(2,1)S(1)}, bf16[1,256,128]{2,0,1:T(2,128)(2,1)S(1)}, u32[]{:S(2)}, u32[]{:S(2)}) %collective-permute-start.4) | collective-permute-done | bytes 65568 | tf_op jit(solution)/shard_map/ppermute | solution.py:16
  44.3 2.9 %collective-permute-done.5 = bf16[1,256,128]{2,0,1:T(2,128)(2,1)S(1)} collective-permute-done((bf16[1,256,128]{2,0,1:T(2,128)(2,1)S(1)}, bf16[1,256,128]{2,0,1:T(2,128)(2,1)S(1)}, u32[]{:S(2)}, u32[]{:S(2)}) %collective-permute-start.5) | collective-permute-done | bytes 65568 | tf_op jit(solution)/shard_map/ppermute | solution.py:17
  51.0 2.3 %collective-permute-done.7 = bf16[34,1,128]{2,0,1:T(8,128)(2,1)S(1)} collective-permute-done((bf16[34,1,128]{2,0,1:T(8,128)(2,1)S(1)}, bf16[34,1,128]{2,0,1:T(8,128)(2,1)S(1)}, u32[]{:S(2)}, u32[]{:S(2)}) %collective-permute-start.7) | collective-permute-done | bytes 8736 | tf_op jit(solution)/shard_map/ppermute | solution.py:17
  55.4 2.6 %fusion.36 = f32[16,8,17,256]{3,1,2,0:T(8,128)S(1)} fusion(bf16[4,4,128,256]{3,2,1,0:T(8,128)(2,1)S(1)} %copy-done.8, bf16[34,1,7,3,128]{4,2,3,0,1:T(8,128)(2,1)S(1)} %slice.78, bf16[34,1,8,34,128]{4,2,3,0,1:T(8,128)(2,1)S(1)} %copy.51, pred[8,17]{0,1:T(8,128)(4,1)S(1)} %copy-done.12), kind=kOutput, calls=%fused_computation.45 | convolution fusion | flops 2289987584 | bytes 5827208 | tf_op jit(solution)/shard_map/conv_general_dilated | solution.py:45
  59.6 2.4 %collective-permute-start.9 = (bf16[1,128,256]{2,0,1:T(2,128)(2,1)S(1)}, bf16[1,128,256]{2,0,1:T(2,128)(2,1)S(1)}, u32[]{:S(2)}, u32[]{:S(2)}) collective-permute-start(bf16[1,128,256]{2,0,1:T(2,128)(2,1)S(1)} %get-tuple-element.24), channel_id=1, source_target_pairs={{4,0},{8,4},{12,8},{16,12},{20,16},{24,20},{28,24},{0,28},{5,1},{9... | collective-permute-start | bytes 196616 | tf_op jit(solution)/shard_map/ppermute | solution.py:17
  62.0 3.6 %collective-permute-done.8 = bf16[1,128,256]{2,0,1:T(2,128)(2,1)S(1)} collective-permute-done((bf16[1,128,256]{2,0,1:T(2,128)(2,1)S(1)}, bf16[1,128,256]{2,0,1:T(2,128)(2,1)S(1)}, u32[]{:S(2)}, u32[]{:S(2)}) %collective-permute-start.8) | collective-permute-done | bytes 65568 | tf_op jit(solution)/shard_map/ppermute | solution.py:16
  65.6 2.3 %collective-permute-done.9 = bf16[1,128,256]{2,0,1:T(2,128)(2,1)S(1)} collective-permute-done((bf16[1,128,256]{2,0,1:T(2,128)(2,1)S(1)}, bf16[1,128,256]{2,0,1:T(2,128)(2,1)S(1)}, u32[]{:S(2)}, u32[]{:S(2)}) %collective-permute-start.9) | collective-permute-done | bytes 65568 | tf_op jit(solution)/shard_map/ppermute | solution.py:17
  71.3 2.3 %collective-permute-done.11 = bf16[18,1,256]{2,0,1:T(8,128)(2,1)S(1)} collective-permute-done((bf16[18,1,256]{2,0,1:T(8,128)(2,1)S(1)}, bf16[18,1,256]{2,0,1:T(8,128)(2,1)S(1)}, u32[]{:S(2)}, u32[]{:S(2)}) %collective-permute-start.11) | collective-permute-done | bytes 9248 | tf_op jit(solution)/shard_map/ppermute | solution.py:17
  81.1 1.8 %copy.63 = bf16[64,64,32]{0,2,1:T(8,128)(2,1)} copy(bf16[64,64,32]{1,2,0:T(8,128)(2,1)S(1)} %bitcast.100) | data formatting | bytes 524288 | tf_op jit(solution)/shard_map/reshape | solution.py:95
  83.0 1.9 %slice.86 = f32[8,64,256]{2,1,0:T(8,128)} slice(f32[8,64,768]{2,1,0:T(8,128)} %get-tuple-element.30), slice={[0:8], [0:64], [0:256]} | slice | bytes 1048576 | tf_op jit(solution)/shard_map/slice | solution.py:90
  87.2 15.6 %all-gather.3.cloned.1.call-done = bf16[64,256,32]{0,2,1:T(8,128)(2,1)} async-done(((bf16[64,64,32]{0,2,1:T(8,128)(2,1)}), bf16[64,256,32]{0,2,1:T(8,128)(2,1)}) %all-gather.3.cloned.1.call-update) | async-done | bytes 1048592 | tf_op jit(solution)/shard_map/all_gather | solution.py:108
  102.8 4.1 %copy.61 = bf16[64,256,32]{1,2,0:T(8,128)(2,1)S(1)} copy(bf16[64,256,32]{0,2,1:T(8,128)(2,1)} %all-gather.3.cloned.1.call-done) | data formatting | bytes 2097152 | tf_op jit(solution)/shard_map/all_gather | solution.py:108
  106.9 2.0 %fusion.89 = (f32[64,64]{1,0:T(8,128)S(1)}, f32[64,64,256]{2,1,0:T(8,128)S(1)}) fusion(bf16[64,64,32]{1,2,0:T(8,128)(2,1)} %bitcast.101, bf16[64,256,32]{1,2,0:T(8,128)(2,1)S(1)} %copy.61), kind=kOutput, calls=%fused_computation.100 | convolution fusion | flops 68153344 | bytes 5521408 | tf_op jit(solution)/shard_map/itd,isd->its/dot_general | solution.py:110
  108.9 1.9 %copy-done.1 = f32[64,64,256]{2,1,0:T(8,128)} copy-done((f32[64,64,256]{2,1,0:T(8,128)}, f32[64,64,256]{2,1,0:T(8,128)S(1)}, u32[]{:S(2)}) %copy-start.1) | copy-done | bytes 4194328
  112.3 14.7 %all-gather.5.cloned.1.call-done = bf16[64,256,32]{0,2,1:T(8,128)(2,1)} async-done(((bf16[64,64,32]{0,2,1:T(8,128)(2,1)}), bf16[64,256,32]{0,2,1:T(8,128)(2,1)}) %all-gather.5.cloned.1.call-update) | async-done | bytes 1048592 | tf_op jit(solution)/shard_map/all_gather | solution.py:109
  127.0 4.1 %copy.64 = bf16[64,256,32]{1,2,0:T(8,128)(2,1)S(1)} copy(bf16[64,256,32]{0,2,1:T(8,128)(2,1)} %all-gather.5.cloned.1.call-done) | data formatting | bytes 2097152 | tf_op jit(solution)/shard_map/all_gather | solution.py:109
  131.1 3.0 %fusion.51 = bf16[64,64,32]{1,2,0:T(8,128)(2,1)S(1)} fusion(bf16[64,256,32]{1,2,0:T(8,128)(2,1)S(1)} %copy.64, f32[64,64,256]{2,1,0:T(8,128)} %copy-done.1, f32[64,64]{1,0:T(8,128)S(1)} %broadcast_maximum_fusion, f32[64,64]{1,0:T(8,128)S(1)} %get-tuple-element.28, f32[64,64]{1,0:T(8,128)S(1)} %get-tuple-element.27), kind=kOutput, calls=%fused_computation.53 | convolution fusion | flops 69599232 | bytes 5554176 | tf_op jit(solution)/shard_map/its,isd->itd/dot_general | solution.py:115
  (89 shorter events, 34.0 us)
Async XLA Ops:
  6.5 68.0 %copy-start = (bf16[4,4,256,256]{3,2,1,0:T(8,128)(2,1)S(1)}, bf16[4,4,256,256]{3,2,1,0:T(8,128)(2,1)}, u32[]{:S(2)}) copy-start(bf16[4,4,256,256]{3,2,1,0:T(8,128)(2,1)} %param.16) | copy-start | bytes 6291460
  6.5 96.3 %all-gather.3.cloned.1.call-start = ((), (), s32[]{:S(2)}) async-start(), calls=%async_computation | async-start | bytes 2621440 | tf_op jit(solution)/shard_map/all_gather | solution.py:108
  12.6 5.3 %collective-permute-start = (bf16[1,96,256]{1,0,2:T(2,128)(2,1)S(1)}, bf16[1,96,256]{1,0,2:T(2,128)(2,1)S(1)}, u32[]{:S(2)}, u32[]{:S(2)}) collective-permute-start(bf16[1,96,256]{1,0,2:T(2,128)(2,1)S(1)} %get-tuple-element.17), channel_id=1, source_target_pairs={{0,4},{4,8},{8,12},{12,16},{16,20},{20,24},{24,28},{28,0},{1,5},{5... | collective-permute-start | bytes 147464 | tf_op jit(solution)/shard_map/ppermute | solution.py:16
  13.9 7.9 %collective-permute-start.1 = (bf16[1,96,256]{1,0,2:T(2,128)(2,1)S(1)}, bf16[1,96,256]{1,0,2:T(2,128)(2,1)S(1)}, u32[]{:S(2)}, u32[]{:S(2)}) collective-permute-start(bf16[1,96,256]{1,0,2:T(2,128)(2,1)S(1)} %get-tuple-element.18), channel_id=1, source_target_pairs={{4,0},{8,4},{12,8},{16,12},{20,16},{24,20},{28,24},{0,28},{5,1},{9... | collective-permute-start | bytes 147464 | tf_op jit(solution)/shard_map/ppermute | solution.py:17
  24.9 2.5 %collective-permute-start.2 = (bf16[34,96,1]{1,0,2:T(8,128)(2,1)S(1)}, bf16[34,96,1]{1,0,2:T(8,128)(2,1)S(1)}, u32[]{:S(2)}, u32[]{:S(2)}) collective-permute-start(bf16[34,96,1]{1,0,2:T(8,128)(2,1)S(1)} %get-tuple-element.9), channel_id=1, source_target_pairs={{0,1},{1,2},{2,3},{3,0},{4,5},{5,6},{6,7},{7,4},{8,9},{9,10},{10,1... | collective-permute-start | bytes 19592 | tf_op jit(solution)/shard_map/ppermute | solution.py:16
  26.5 3.1 %collective-permute-start.3 = (bf16[34,96,1]{1,0,2:T(8,128)(2,1)S(1)}, bf16[34,96,1]{1,0,2:T(8,128)(2,1)S(1)}, u32[]{:S(2)}, u32[]{:S(2)}) collective-permute-start(bf16[34,96,1]{1,0,2:T(8,128)(2,1)S(1)} %get-tuple-element.10), channel_id=1, source_target_pairs={{1,0},{2,1},{3,2},{0,3},{5,4},{6,5},{7,6},{4,7},{9,8},{10,9},{11,1... | collective-permute-start | bytes 19592 | tf_op jit(solution)/shard_map/ppermute | solution.py:17
  30.9 0.9 copy-start.9
  38.6 5.7 %collective-permute-start.4 = (bf16[1,256,128]{2,0,1:T(2,128)(2,1)S(1)}, bf16[1,256,128]{2,0,1:T(2,128)(2,1)S(1)}, u32[]{:S(2)}, u32[]{:S(2)}) collective-permute-start(bf16[1,256,128]{2,0,1:T(2,128)(2,1)S(1)} %get-tuple-element.15), channel_id=1, source_target_pairs={{0,4},{4,8},{8,12},{12,16},{16,20},{20,24},{24,28},{28,0},{1,5},{5... | collective-permute-start | bytes 196616 | tf_op jit(solution)/shard_map/ppermute | solution.py:16
  39.0 8.2 %collective-permute-start.5 = (bf16[1,256,128]{2,0,1:T(2,128)(2,1)S(1)}, bf16[1,256,128]{2,0,1:T(2,128)(2,1)S(1)}, u32[]{:S(2)}, u32[]{:S(2)}) collective-permute-start(bf16[1,256,128]{2,0,1:T(2,128)(2,1)S(1)} %get-tuple-element.16), channel_id=1, source_target_pairs={{4,0},{8,4},{12,8},{16,12},{20,16},{24,20},{28,24},{0,28},{5,1},{9... | collective-permute-start | bytes 196616 | tf_op jit(solution)/shard_map/ppermute | solution.py:17
  48.9 2.1 %collective-permute-start.6 = (bf16[34,1,128]{2,0,1:T(8,128)(2,1)S(1)}, bf16[34,1,128]{2,0,1:T(8,128)(2,1)S(1)}, u32[]{:S(2)}, u32[]{:S(2)}) collective-permute-start(bf16[34,1,128]{2,0,1:T(8,128)(2,1)S(1)} %get-tuple-element.7), channel_id=1, source_target_pairs={{0,1},{1,2},{2,3},{3,0},{4,5},{5,6},{6,7},{7,4},{8,9},{9,10},{10,1... | collective-permute-start | bytes 26120 | tf_op jit(solution)/shard_map/ppermute | solution.py:16
  50.1 3.1 %collective-permute-start.7 = (bf16[34,1,128]{2,0,1:T(8,128)(2,1)S(1)}, bf16[34,1,128]{2,0,1:T(8,128)(2,1)S(1)}, u32[]{:S(2)}, u32[]{:S(2)}) collective-permute-start(bf16[34,1,128]{2,0,1:T(8,128)(2,1)S(1)} %get-tuple-element.8), channel_id=1, source_target_pairs={{1,0},{2,1},{3,2},{0,3},{5,4},{6,5},{7,6},{4,7},{9,8},{10,9},{11,1... | collective-permute-start | bytes 26120 | tf_op jit(solution)/shard_map/ppermute | solution.py:17
  54.2 1.2 copy-start.8
  54.2 1.2 copy-start.12
  59.6 6.0 %collective-permute-start.8 = (bf16[1,128,256]{2,0,1:T(2,128)(2,1)S(1)}, bf16[1,128,256]{2,0,1:T(2,128)(2,1)S(1)}, u32[]{:S(2)}, u32[]{:S(2)}) collective-permute-start(bf16[1,128,256]{2,0,1:T(2,128)(2,1)S(1)} %get-tuple-element.23), channel_id=1, source_target_pairs={{0,4},{4,8},{8,12},{12,16},{16,20},{20,24},{24,28},{28,0},{1,5},{5... | collective-permute-start | bytes 196616 | tf_op jit(solution)/shard_map/ppermute | solution.py:16
  59.6 8.2 %collective-permute-start.9 = (bf16[1,128,256]{2,0,1:T(2,128)(2,1)S(1)}, bf16[1,128,256]{2,0,1:T(2,128)(2,1)S(1)}, u32[]{:S(2)}, u32[]{:S(2)}) collective-permute-start(bf16[1,128,256]{2,0,1:T(2,128)(2,1)S(1)} %get-tuple-element.24), channel_id=1, source_target_pairs={{4,0},{8,4},{12,8},{16,12},{20,16},{24,20},{28,24},{0,28},{5,1},{9... | collective-permute-start | bytes 196616 | tf_op jit(solution)/shard_map/ppermute | solution.py:17
  69.0 2.3 %collective-permute-start.10 = (bf16[18,1,256]{2,0,1:T(8,128)(2,1)S(1)}, bf16[18,1,256]{2,0,1:T(8,128)(2,1)S(1)}, u32[]{:S(2)}, u32[]{:S(2)}) collective-permute-start(bf16[18,1,256]{2,0,1:T(8,128)(2,1)S(1)} %get-tuple-element.19), channel_id=1, source_target_pairs={{0,1},{1,2},{2,3},{3,0},{4,5},{5,6},{6,7},{7,4},{8,9},{9,10},{10,1... | collective-permute-start | bytes 27656 | tf_op jit(solution)/shard_map/ppermute | solution.py:16
  70.4 3.1 %collective-permute-start.11 = (bf16[18,1,256]{2,0,1:T(8,128)(2,1)S(1)}, bf16[18,1,256]{2,0,1:T(8,128)(2,1)S(1)}, u32[]{:S(2)}, u32[]{:S(2)}) collective-permute-start(bf16[18,1,256]{2,0,1:T(8,128)(2,1)S(1)} %get-tuple-element.20), channel_id=1, source_target_pairs={{1,0},{2,1},{3,2},{0,3},{5,4},{6,5},{7,6},{4,7},{9,8},{10,9},{11,1... | collective-permute-start | bytes 27656 | tf_op jit(solution)/shard_map/ppermute | solution.py:17
  74.6 1.7 %copy-start.5 = (f32[256]{0:T(256)S(1)}, f32[256]{0:T(256)}, u32[]{:S(2)}) copy-start(f32[256]{0:T(256)} %param.17) | copy-start | bytes 3076
  76.0 1.0 copy-start.2
  76.0 1.0 copy-start.6
  78.6 4.4 %copy-start.10 = (f32[8]{0:T(128)S(1)}, f32[8]{0:T(128)}, u32[]{:S(2)}) copy-start(f32[8]{0:T(128)} %param.20) | copy-start | bytes 100
  80.8 46.2 %all-gather.5.cloned.1.call-start = ((), (), s32[]{:S(2)}) async-start(), calls=%async_computation.1 | async-start | bytes 2621440 | tf_op jit(solution)/shard_map/all_gather | solution.py:109
  108.9 2.0 %copy-start.1 = (f32[64,64,256]{2,1,0:T(8,128)}, f32[64,64,256]{2,1,0:T(8,128)S(1)}, u32[]{:S(2)}) copy-start(f32[64,64,256]{2,1,0:T(8,128)S(1)} %get-tuple-element.32) | copy-start | bytes 12582916
  131.1 3.1 %copy-start.3 = (bf16[256,256]{1,0:T(8,128)(2,1)S(1)}, bf16[256,256]{1,0:T(8,128)(2,1)}, u32[]{:S(2)}) copy-start(bf16[256,256]{1,0:T(8,128)(2,1)} %param.21) | copy-start | bytes 393220
  (4 other events, 3.2 us)
Sparse Core Ops, SparseCore 0:
  80.9 21.8 all-gather.2
  104.4 22.5 all-gather.4
where the time goes:
time: 144 us; the launch traced here: 142 us
  waiting for transfers between devices  58.4 us (41%)
  local copies, waits for them, and re-layouts  29.9 us (21%)
  matrix products  16.2 us (11%)
  between operations  13.9 us (10%)
  other arithmetic  11.9 us (8%)
  starting transfers between devices  11.7 us (8%)
    ppermute x6, waiting for transfers between devices, extended_2(): after = lax.ppermute(initial, axis, down)  16 us
    all_gather x1, waiting for transfers between devices, on_device(): key_part = lax.all_gather(key_items, 'lon', axis=1, tiled=True)  15.6 us
    all_gather x1, waiting for transfers between devices, on_device(): value_part = lax.all_gather(value_items, 'lon', axis=1, tiled=True)  14.7 us
    ppermute x6, waiting for transfers between devices, extended_2(): before = lax.ppermute(last, axis, up)  12.1 us
    unnamed x29, local copies, waits for them, and re-layouts  7.85 us
    ppermute x6, starting transfers between devices, extended_2(): before = lax.ppermute(last, axis, up)  6.11 us
    concatenate x3, other arithmetic, extended_2(): value = jnp.concatenate([before, value, after], axis=dim)  5.82 us
    ppermute x6, starting transfers between devices, extended_2(): after = lax.ppermute(initial, axis, down)  5.51 us
  transfers between devices with their start and end apart: 14, of which 14 were waited for; matrix products, arithmetic and copies ran while one was open for 10% of the time, Pallas kernels for 0%

commit v1 on v0

v1 whole, which is shorter than its diff:
```python
import functools

import jax
import jax.numpy as jnp
from jax import lax
from jax.experimental import pallas as pl
from jax.experimental.pallas import tpu as pltpu
from jax.sharding import PartitionSpec as P

HEADS = 8
HALO = 4
BF = jnp.bfloat16
F32 = jnp.float32


def silu(v):
    half = 0.5 * v
    return half + half * jnp.tanh(half)


def dot(a, b):
    return jnp.dot(a, b, preferred_element_type=F32)


def build_first_kernel(taps_ref, w1):
    cin, cout = taps_ref.shape[2:]
    w1[...] = jnp.zeros_like(w1)
    for dy in range(3):
        for col in range(4):
            for out in range(2):
                if 0 <= col - out < 3:
                    w1[dy, col * 128 : col * 128 + cin, out * cout : (out + 1) * cout] = taps_ref[
                        dy, col - out
                    ]


def spread_row(value, left, right, xt, slot, xa, row, wide):
    cin, cols = value.shape
    xt[slot, HALO : HALO + cols, 0:cin] = value.astype(F32).T
    xt[slot, 0:HALO, :] = left.astype(F32)
    xt[slot, HALO + cols : 2 * HALO + cols, :] = right.astype(F32)
    for phase in range(6):
        part = xt[slot, pl.ds(phase, wide, 4), :]
        xa[pl.ds(row * wide, wide), phase * 128 : (phase + 1) * 128] = part.astype(BF)


def conv_kernel(
    wide, x_ref, top_ref, bottom_ref, left_ref, right_ref, taps_ref, b1_ref, w2_ref, b2_ref, w3_ref,
    b3_ref, out_ref, w1, xt, xa, first, second,
):
    lat = lax.axis_index("lat")
    bands = lax.axis_size("lat")
    rows, cin, cols = x_ref.shape
    tokens = cols // 4
    build_first_kernel(taps_ref, w1)
    xt[...] = jnp.zeros_like(xt)

    def own(step, carry):
        for k in range(4):
            r = step * 4 + k
            spread_row(
                x_ref[r], left_ref[r + HALO], right_ref[r + HALO], xt, k, xa, r + HALO, wide
            )
        return carry

    lax.fori_loop(0, rows // 4, own, 0)
    for k in range(HALO):
        spread_row(top_ref[k], left_ref[k], right_ref[k], xt, k, xa, k, wide)
    for k in range(HALO):
        r = rows + HALO + k
        spread_row(bottom_ref[k], left_ref[r], right_ref[r], xt, k, xa, r, wide)

    @pl.when(lat == 0)
    def _():
        xa[0 : HALO * wide, :] = jnp.zeros((HALO * wide, xa.shape[1]), BF)

    @pl.when(lat == bands - 1)
    def _():
        xa[(rows + HALO) * wide :, :] = jnp.zeros((HALO * wide, xa.shape[1]), BF)

    bias1 = jnp.concatenate([b1_ref[...], b1_ref[...]], axis=1)

    def conv1(step, carry):
        pair = []
        for side in range(2):
            total = bias1
            for dy in range(3):
                lhs = xa[
                    pl.ds((2 * step + dy) * wide, 2 * wide), side * 256 : side * 256 + 512
                ]
                total = total + dot(lhs, w1[dy])
            pair.append(silu(total))
        for k in range(2):
            row = lat * rows + 2 * step + k - 3
            inside = (row >= 0) & (row < bands * rows)
            where = pl.ds(step * wide, wide)
            a = jnp.where(inside, pair[0][k * wide : (k + 1) * wide], 0.0)
            b = jnp.where(inside, pair[1][k * wide : (k + 1) * wide], 0.0)
            first[k, where, 0:256] = a.astype(BF)
            first[k, where, 256:512] = b.astype(BF)
            first[k, where, 512:768] = pltpu.roll(a, wide - 1, 0).astype(BF)
        return carry

    lax.fori_loop(0, (rows + 6) // 2, conv1, 0)

    half = rows // 2

    def conv2(step, carry):
        sides = []
        for side in range(2):
            total = b2_ref[...]
            for dy in range(4):
                lhs = first[
                    dy % 2,
                    pl.ds((2 * step + dy // 2) * wide, 2 * wide),
                    side * 256 : side * 256 + 512,
                ]
                total = total + dot(lhs, w2_ref[dy])
            sides.append(silu(total))
        for k in range(2):
            row = lat * half + 2 * step + k - 1
            inside = (row >= 0) & (row < bands * half)
            where = pl.ds(step * tokens, tokens)
            for side in range(2):
                a = jnp.where(inside, sides[side][k * wide : (k + 1) * wide], 0.0)
                second[k, where, side * 256 : side * 256 + 256] = a[:tokens].astype(BF)
                second[k, where, 512 + side * 256 : 768 + side * 256] = pltpu.roll(
                    a, wide - 1, 0
                )[:tokens].astype(BF)
        return carry

    lax.fori_loop(0, (half + 2) // 2, conv2, 0)

    final = rows // 4
    part = final // 2

    def conv3(step, carry):
        total = b3_ref[...]
        for dy in range(4):
            lhs = second[dy % 2, pl.ds((step * part + dy // 2) * tokens, part * tokens), :]
            total = total + dot(lhs, w3_ref[dy])
        out_ref[pl.ds(step * part, part)] = (
            silu(total).astype(BF).reshape(part, tokens, total.shape[1])
        )
        return carry

    lax.fori_loop(0, 2, conv3, 0)


def attention_kernel(f_ref, gain_ref, wqkv_ref, sharp_ref, wo_ref, out_ref, qs, ks, vs, att):
    rows, tokens, width = f_ref.shape
    depth = width // HEADS
    feats = f_ref[...].reshape(rows * tokens, width).astype(F32)
    mean = jnp.mean(feats, axis=-1, keepdims=True)
    centred = feats - mean
    variance = jnp.mean(centred * centred, axis=-1, keepdims=True)
    normed = (centred * lax.rsqrt(variance + 1e-05) * gain_ref[...]).astype(BF)
    lane = lax.broadcasted_iota(jnp.int32, (1, width), 1)
    scale = jnp.zeros((1, width), F32)
    for h in range(HEADS):
        mine = (lane >= h * depth) & (lane < (h + 1) * depth)
        scale = jnp.where(mine, sharp_ref[h] / jnp.sqrt(F32(depth)), scale)
    qs[...] = (dot(normed, wqkv_ref[:, :width]) * scale).astype(BF)
    ks[...] = dot(normed, wqkv_ref[:, width : 2 * width]).astype(BF)
    vs[...] = dot(normed, wqkv_ref[:, 2 * width :]).astype(BF)
    block = min(256, tokens)
    per_row = tokens // block

    def body(step, carry):
        row = step // per_row
        q = qs[pl.ds(step * block, block), :]
        k = ks[pl.ds(row * tokens, tokens), :]
        v = vs[pl.ds(row * tokens, tokens), :]
        joined = jnp.zeros((block, width), F32)
        for h in range(HEADS):
            mine = (lane >= h * depth) & (lane < (h + 1) * depth)
            masked = jnp.where(mine, q.astype(F32), 0.0).astype(BF)
            scores = lax.dot_general(
                masked, k, (((1,), (1,)), ((), ())), preferred_element_type=F32
            )
            weights = jnp.exp(scores - jnp.max(scores, axis=-1, keepdims=True))
            total = jnp.sum(weights, axis=-1, keepdims=True)
            summed = dot(weights.astype(BF), v)
            joined = jnp.where(mine, summed / total, joined)
        att[pl.ds(step * block, block), :] = joined.astype(BF)
        return carry

    lax.fori_loop(0, rows * per_row, body, 0)
    mixed = dot(att[...], wo_ref[...])
    out_ref[...] = (feats + mixed).astype(BF).reshape(rows, tokens, width)


VM = pl.BlockSpec(memory_space=pltpu.VMEM)
SM = pl.BlockSpec(memory_space=pltpu.SMEM)


def on_device(x, taps1, b1, taps2, b2, taps3, b3, gain, wqkv, sharp, wo):
    rows, cin, cols = x.shape
    tokens = cols // 4
    bands, sectors = lax.axis_size("lat"), lax.axis_size("lon")
    width = taps3.shape[3]
    wide = -(-(tokens + 2) // 16) * 16

    def ring(axis, size, last, initial):
        up = [(i, (i + 1) % size) for i in range(size)]
        down = [(j, i) for i, j in up]
        return lax.ppermute(last, axis, up), lax.ppermute(initial, axis, down)

    top, bottom = ring("lat", bands, x[-HALO:], x[:HALO])

    def edge(a):
        b = jnp.concatenate([top[:, :, a], x[:, :, a], bottom[:, :, a]], axis=0)
        return jnp.pad(jnp.transpose(b, (0, 2, 1)), ((0, 0), (0, 0), (0, 128 - cin)))

    left, right = ring("lon", sectors, edge(slice(cols - HALO, cols)), edge(slice(0, HALO)))
    features = pl.pallas_call(
        functools.partial(conv_kernel, wide),
        out_shape=jax.ShapeDtypeStruct((rows // 4, tokens, width), BF),
        in_specs=[VM] * 11,
        out_specs=VM,
        scratch_shapes=[
            pltpu.VMEM((3, 512, 256), BF),
            pltpu.VMEM((4, 4 * wide + 8, 128), F32),
            pltpu.VMEM(((rows + 2 * HALO) * wide, 768), BF),
            pltpu.VMEM((2, (rows + 6) // 2 * wide, 768), BF),
            pltpu.VMEM((2, (rows // 2 + 2) // 2 * tokens, 1024), BF),
        ],
        compiler_params=pltpu.CompilerParams(vmem_limit_bytes=56 * 2**20),
        name="convs",
    )(
        x, top, bottom, left, right, taps1, b1[None], taps2.reshape(4, -1, width), b2[None],
        taps3.reshape(4, -1, width), b3[None],
    )
    copies = max(1, sectors // features.shape[0])
    if copies > 1:
        features = jnp.repeat(features, copies, axis=0)
    whole_rows = lax.all_to_all(features, "lon", 0, 1, tiled=True)
    n = whole_rows.shape[0] * whole_rows.shape[1]
    encoded = pl.pallas_call(
        attention_kernel,
        out_shape=jax.ShapeDtypeStruct(whole_rows.shape, BF),
        in_specs=[VM, VM, VM, SM, VM],
        out_specs=VM,
        scratch_shapes=[pltpu.VMEM((n, width), BF)] * 4,
        compiler_params=pltpu.CompilerParams(vmem_limit_bytes=56 * 2**20),
        name="attention",
    )(whole_rows, gain[None], wqkv, sharp, wo)
    return lax.all_to_all(encoded, "lon", 1, 0, tiled=True)[::copies]


def solution(mesh):
    return jax.shard_map(
        on_device,
        mesh=mesh,
        in_specs=(P("lat", None, "lon"), P(), P(), P(), P(), P(), P(), P(), P(), P(), P()),
        out_specs=P("lat", "lon", None),
        check_vma=False,
    )
```

time: 144 us -> 72.6 us (0.50)
  the two profiles are of different devices: /device:TPU:17 before, /device:TPU:0 now
where the time goes in v1:
time: 72.6 us; the launch traced here: 72.3 us
  Pallas kernels  26.3 us (36%)
  blocking collectives  17.8 us (25%)
  local copies, waits for them, and re-layouts  10.5 us (14%)
  waiting for transfers between devices  9.59 us (13%)
  starting transfers between devices  7.8 us (11%)
    pallas_call x1, Pallas kernels, on_device(): pl.pallas_call(functools.partial(conv_kernel, wide), out_shape=jax.ShapeD...  21.4 us
    ppermute x4, waiting for transfers between devices, ring(): return (lax.ppermute(last, axis, up), lax.ppermute(initial, axis, down))  9.59 us
    all_to_all x1, blocking collectives, on_device(): whole_rows = lax.all_to_all(features, 'lon', 0, 1, tiled=True)  9.41 us
    all_to_all x1, blocking collectives, on_device(): return lax.all_to_all(encoded, 'lon', 1, 0, tiled=True)[::copies]  8.42 us
    ppermute x4, starting transfers between devices, ring(): return (lax.ppermute(last, axis, up), lax.ppermute(initial, axis, down))  7.8 us
    pallas_call x1, Pallas kernels, on_device(): pl.pallas_call(attention_kernel, out_shape=jax.ShapeDtypeStruct(whole_row...  4.96 us
    unnamed x10, local copies, waits for them, and re-layouts  3 us
    ppermute x2, local copies, waits for them, and re-layouts, ring(): return (lax.ppermute(last, axis, up), lax.ppermute(initial, axis, down))  2.56 us
  transfers between devices with their start and end apart: 4, of which 2 were waited for; matrix products, arithmetic and copies ran while one was open for 6% of the time, Pallas kernels for 0%

profile of v1, /device:TPU:0, one launch (start us, length us, event | category | flops | bytes accessed | tf_op | source)
XLA Modules:
  0.0 72.3 jit_solution(8555114987710778127)
XLA Ops:
  0.0 1.2 %fusion.1 = (bf16[4,96,256]{2,1,0:T(8,128)(2,1)S(1)}, bf16[4,96,256]{2,1,0:T(8,128)(2,1)S(1)}) fusion(bf16[32,96,256]{2,1,0:T(8,128)(2,1)} %x_ref.1), kind=kLoop, calls=%fused_computation.3 | loop fusion | bytes 786432 | tf_op jit(solution)/shard_map/slice | solution.py:209
  1.2 0.8 %copy.29 = bf16[4,96,256]{1,2,0:T(8,128)(2,1)} copy(bf16[4,96,256]{2,1,0:T(8,128)(2,1)S(1)} %get-tuple-element.8) | data formatting | bytes 393216
  2.0 3.0 %collective-permute-start = (bf16[4,96,256]{1,2,0:T(8,128)(2,1)}, bf16[4,96,256]{1,2,0:T(8,128)(2,1)S(1)}, u32[]{:S(2)}, u32[]{:S(2)}) collective-permute-start(bf16[4,96,256]{1,2,0:T(8,128)(2,1)} %copy.29), channel_id=1, source_target_pairs={{0,4},{4,8},{8,12},{12,16},{16,20},{20,24},{24,28},{28,0},{1,5},{5... | collective-permute-start | bytes 589832 | tf_op jit(solution)/shard_map/ppermute | solution.py:207
  5.0 0.8 %copy.30 = bf16[4,96,256]{1,2,0:T(8,128)(2,1)} copy(bf16[4,96,256]{2,1,0:T(8,128)(2,1)S(1)} %get-tuple-element.7) | data formatting | bytes 393216
  5.8 3.0 %collective-permute-start.1 = (bf16[4,96,256]{1,2,0:T(8,128)(2,1)}, bf16[4,96,256]{1,2,0:T(8,128)(2,1)}, u32[]{:S(2)}, u32[]{:S(2)}) collective-permute-start(bf16[4,96,256]{1,2,0:T(8,128)(2,1)} %copy.30), channel_id=1, source_target_pairs={{4,0},{8,4},{12,8},{16,12},{20,16},{24,20},{28,24},{0,28},{5,1},{9... | collective-permute-start | bytes 589832 | tf_op jit(solution)/shard_map/ppermute | solution.py:207
  8.9 0.4 fusion
  9.2 0.3 copy.32
  9.6 0.3 copy.31
  9.9 6.6 %collective-permute-done = bf16[4,96,256]{1,2,0:T(8,128)(2,1)S(1)} collective-permute-done((bf16[4,96,256]{1,2,0:T(8,128)(2,1)}, bf16[4,96,256]{1,2,0:T(8,128)(2,1)S(1)}, u32[]{:S(2)}, u32[]{:S(2)}) %collective-permute-start) | collective-permute-done | bytes 196640 | tf_op jit(solution)/shard_map/ppermute | solution.py:207
  16.5 3.0 %collective-permute-done.1 = bf16[4,96,256]{1,2,0:T(8,128)(2,1)} collective-permute-done((bf16[4,96,256]{1,2,0:T(8,128)(2,1)}, bf16[4,96,256]{1,2,0:T(8,128)(2,1)}, u32[]{:S(2)}, u32[]{:S(2)}) %collective-permute-start.1) | collective-permute-done | bytes 196640 | tf_op jit(solution)/shard_map/ppermute | solution.py:207
  19.5 0.7 fusion.3
  20.4 0.1 collective-permute-start.2
  20.5 1.7 %collective-permute-start.3 = (bf16[40,4,128]{2,1,0:T(4,128)(2,1)S(1)}, bf16[40,4,128]{2,1,0:T(4,128)(2,1)S(1)}, u32[]{:S(2)}, u32[]{:S(2)}) collective-permute-start(bf16[40,4,128]{2,1,0:T(4,128)(2,1)S(1)} %pad.8), channel_id=1, source_target_pairs={{1,0},{2,1},{3,2},{0,3},{5,4},{6,5},{7,6},{4,7},{9,8},{10,9},{11,1... | collective-permute-start | bytes 122888 | tf_op jit(solution)/shard_map/ppermute | solution.py:207
  22.2 0.8 %copy.24.top_ref = bf16[4,96,256]{2,1,0:T(8,128)(2,1)} copy(bf16[4,96,256]{1,2,0:T(8,128)(2,1)S(1)} %collective-permute-done) | data formatting | bytes 393216 | tf_op jit(solution)/shard_map/ppermute | solution.py:207
  23.0 1.7 %copy.25.bottom_ref = bf16[4,96,256]{2,1,0:T(8,128)(2,1)} copy(bf16[4,96,256]{1,2,0:T(8,128)(2,1)} %collective-permute-done.1) | data formatting | bytes 393216 | tf_op jit(solution)/shard_map/ppermute | solution.py:207
  24.8 0.6 copy-done.1
  25.4 0.0 copy-done.2
  25.4 21.4 %convs.1 = bf16[8,64,256]{2,1,0:T(8,128)(2,1)} custom-call(bf16[32,96,256]{2,1,0:T(8,128)(2,1)} %x_ref.1, bf16[4,96,256]{2,1,0:T(8,128)(2,1)} %copy.24.top_ref, bf16[4,96,256]{2,1,0:T(8,128)(2,1)} %copy.25.bottom_ref, bf16[40,4,128]{2,1,0:T(4,128)(2,1)} %copy-done.1, bf16[40,4,128]{2,1,0:T(4,128)(2,1)} %copy-done.2, bf16[3,3,96,128]{3,2,1,0:T(8,128)(2,1)} %taps_ref.1, ...), custom_call_target="tpu_custom_call" | custom-call | tf_op jit(solution)/shard_map/convs/pallas_call | solution.py:216
  46.8 9.4 %all_to_all.36 = bf16[8,64,256]{2,1,0:T(8,128)(2,1)S(1)} all-to-all(bf16[8,64,256]{2,1,0:T(8,128)(2,1)} %convs.1), channel_id=1, replica_groups=mesh['lat'=8,'lon'=4] {'lon'}, dimensions={0} | all-to-all | bytes 524288 | tf_op jit(solution)/shard_map/all_to_all | solution.py:237
  56.2 0.7 copy.26
  56.9 5.0 %attention.1 = bf16[2,256,256]{2,1,0:T(8,128)(2,1)} custom-call(bf16[2,256,256]{2,1,0:T(8,128)(2,1)} %bitcast.19, f32[1,256]{1,0:T(1,128)} %bitcast.23, bf16[256,768]{1,0:T(8,128)(2,1)} %wqkv_ref.1, f32[8]{0:T(128)} %sharp_ref.1, bf16[256,256]{1,0:T(8,128)(2,1)} %wo_ref.1), custom_call_target="tpu_custom_call" | custom-call | tf_op jit(solution)/shard_map/attention/pallas_call | solution.py:239
  61.9 1.2 %copy.27 = bf16[2,256,256]{2,0,1:T(2,128)(2,1)S(1)} copy(bf16[2,256,256]{2,1,0:T(8,128)(2,1)} %attention.1) | data formatting | bytes 524288 | tf_op jit(solution)/shard_map/attention/pallas_call | solution.py:239
  63.1 8.4 %all_to_all.37 = bf16[2,256,256]{2,0,1:T(2,128)(2,1)S(1)} all-to-all(bf16[2,256,256]{2,0,1:T(2,128)(2,1)S(1)} %copy.27), channel_id=1, replica_groups=mesh['lat'=8,'lon'=4] {'lon'}, dimensions={1} | all-to-all | bytes 524288 | tf_op jit(solution)/shard_map/all_to_all | solution.py:248
  71.5 0.7 %copy.28 = bf16[4,2,64,256]{3,2,1,0:T(8,128)(2,1)} copy(bf16[4,2,64,256]{3,1,2,0:T(2,128)(2,1)S(1)} %bitcast.21) | data formatting | bytes 524288 | tf_op jit(solution)/shard_map/all_to_all | solution.py:248
  (11 shorter events, 0.2 us)
Async XLA Ops:
  0.0 8.9 %copy-start = (bf16[32,96,256]{2,1,0:T(8,128)(2,1)S(1)}, bf16[32,96,256]{2,1,0:T(8,128)(2,1)}, u32[]{:S(2)}) copy-start(bf16[32,96,256]{2,1,0:T(8,128)(2,1)} %x_ref.1) | copy-start | bytes 4718596
  2.0 14.5 %collective-permute-start = (bf16[4,96,256]{1,2,0:T(8,128)(2,1)}, bf16[4,96,256]{1,2,0:T(8,128)(2,1)S(1)}, u32[]{:S(2)}, u32[]{:S(2)}) collective-permute-start(bf16[4,96,256]{1,2,0:T(8,128)(2,1)} %copy.29), channel_id=1, source_target_pairs={{0,4},{4,8},{8,12},{12,16},{16,20},{20,24},{24,28},{28,0},{1,5},{5... | collective-permute-start | bytes 589832 | tf_op jit(solution)/shard_map/ppermute | solution.py:207
  5.8 13.7 %collective-permute-start.1 = (bf16[4,96,256]{1,2,0:T(8,128)(2,1)}, bf16[4,96,256]{1,2,0:T(8,128)(2,1)}, u32[]{:S(2)}, u32[]{:S(2)}) collective-permute-start(bf16[4,96,256]{1,2,0:T(8,128)(2,1)} %copy.30), channel_id=1, source_target_pairs={{4,0},{8,4},{12,8},{16,12},{20,16},{24,20},{28,24},{0,28},{5,1},{9... | collective-permute-start | bytes 589832 | tf_op jit(solution)/shard_map/ppermute | solution.py:207
  20.4 4.4 %collective-permute-start.2 = (bf16[40,4,128]{2,1,0:T(4,128)(2,1)S(1)}, bf16[40,4,128]{2,1,0:T(4,128)(2,1)S(1)}, u32[]{:S(2)}, u32[]{:S(2)}) collective-permute-start(bf16[40,4,128]{2,1,0:T(4,128)(2,1)S(1)} %pad.7), channel_id=1, source_target_pairs={{0,1},{1,2},{2,3},{3,0},{4,5},{5,6},{6,7},{7,4},{8,9},{9,10},{10,1... | collective-permute-start | bytes 122888 | tf_op jit(solution)/shard_map/ppermute | solution.py:207
  20.5 4.3 %collective-permute-start.3 = (bf16[40,4,128]{2,1,0:T(4,128)(2,1)S(1)}, bf16[40,4,128]{2,1,0:T(4,128)(2,1)S(1)}, u32[]{:S(2)}, u32[]{:S(2)}) collective-permute-start(bf16[40,4,128]{2,1,0:T(4,128)(2,1)S(1)} %pad.8), channel_id=1, source_target_pairs={{1,0},{2,1},{3,2},{0,3},{5,4},{6,5},{7,6},{4,7},{9,8},{10,9},{11,1... | collective-permute-start | bytes 122888 | tf_op jit(solution)/shard_map/ppermute | solution.py:207
  24.8 0.6 copy-start.1
  24.8 0.6 copy-start.2

commit v2 on v1

v2 whole, which is shorter than its diff:
```python
import functools

import jax
import jax.numpy as jnp
from jax import lax
from jax.experimental import pallas as pl
from jax.experimental.pallas import tpu as pltpu
from jax.sharding import PartitionSpec as P

HEADS = 8
HALO = 4
BF = jnp.bfloat16
F32 = jnp.float32


def silu(v):
    half = 0.5 * v
    return half + half * jnp.tanh(half)


def dot(a, b):
    return jnp.dot(a, b, preferred_element_type=F32)


def build_first_kernel(taps_ref, w1):
    cin, cout = taps_ref.shape[2:]
    w1[...] = jnp.zeros_like(w1)
    for dy in range(3):
        for col in range(4):
            for out in range(2):
                if 0 <= col - out < 3:
                    w1[dy, col * 128 : col * 128 + cin, out * cout : (out + 1) * cout] = taps_ref[
                        dy, col - out
                    ]


def turned(value):
    cin, cols = value.shape
    zeros = jnp.zeros((128 - cin, cols), F32)
    return jnp.concatenate([value.astype(F32), zeros], axis=0).T


def remote(src, dst, send, recv, lat, lon):
    return pltpu.make_async_remote_copy(
        src_ref=src, dst_ref=dst, send_sem=send, recv_sem=recv, device_id=(lat, lon),
        device_id_type=pl.DeviceIdType.MESH,
    )


def kernel(
    wide, x_ref, taps_ref, b1_ref, w2_hbm, b2_ref, w3_hbm, b3_ref, gain_ref, wqkv_hbm, sharp_ref,
    wo_hbm, out_ref, w2_ref, w3_ref, wqkv_ref, wo_ref, w1, top, bottom, edges, rims, xt, xa, first,
    second, local, whole, qs, ks, vs, att, enc, landed, weight_sem, row_sem, edge_send, edge_recv,
    go_send, go_recv, back_send, back_recv,
):
    lat, lon = lax.axis_index("lat"), lax.axis_index("lon")
    bands, sectors = lax.axis_size("lat"), lax.axis_size("lon")
    rows, cin, cols = x_ref.shape
    tokens = cols // 4
    groups = rows // 4
    has_up, has_down = lat > 0, lat < bands - 1
    up, down = jnp.maximum(lat - 1, 0), jnp.minimum(lat + 1, bands - 1)
    west, east = lax.rem(lon + sectors - 1, sectors), lax.rem(lon + 1, sectors)
    both = ((has_up, up), (has_down, down))

    weights = [
        pltpu.make_async_copy(src, dst, weight_sem.at[i])
        for i, (src, dst) in enumerate(
            ((w2_hbm, w2_ref), (w3_hbm, w3_ref), (wqkv_hbm, wqkv_ref), (wo_hbm, wo_ref))
        )
    ]

    barrier = pltpu.get_barrier_semaphore()

    def greet(to_lat, to_lon):
        pl.semaphore_signal(
            barrier, inc=1, device_id=(to_lat, to_lon), device_id_type=pl.DeviceIdType.MESH
        )

    for step in range(1, sectors):
        greet(lat, lax.rem(lon + step, sectors))
    for there, other in both:
        @pl.when(there)
        def _():
            greet(other, lon)
            greet(other, west)
            greet(other, east)

    for copy in weights:
        copy.start()
    build_first_kernel(taps_ref, w1)
    for r in range(rows + 2 * HALO):
        xt[r, 2 * HALO + cols :, :] = jnp.zeros((xt.shape[1] - cols - 2 * HALO, 128), F32)

    peers = sectors - 1 + jnp.where(has_up, 3, 0) + jnp.where(has_down, 3, 0)
    pl.semaphore_wait(barrier, peers)

    to_up = remote(x_ref.at[0:HALO], bottom, row_sem.at[0], row_sem.at[2], up, lon)
    to_down = remote(
        x_ref.at[rows - HALO : rows], top, row_sem.at[1], row_sem.at[3], down, lon
    )

    @pl.when(has_up)
    def _():
        to_up.start()

    @pl.when(has_down)
    def _():
        to_down.start()

    def own(step, carry):
        initial, last = [], []
        for k in range(4):
            r = step * 4 + k
            value = turned(x_ref[r])
            xt[r + HALO, HALO : HALO + cols, :] = value
            initial.append(value[:HALO])
            last.append(value[cols - HALO :])
        edges[0, step] = jnp.concatenate(initial, axis=0).astype(BF)
        edges[1, step] = jnp.concatenate(last, axis=0).astype(BF)
        return carry

    lax.fori_loop(0, groups, own, 0)

    rim_copies = []
    for side, to_lon in ((0, west), (1, east)):
        slot = 3 * side
        target = 1 - side
        rim_copies.append(
            (None, None, remote(
                edges.at[side], rims.at[target, pl.ds(1, groups)], edge_send.at[slot],
                edge_recv.at[slot], lat, to_lon,
            ))
        )
        rim_copies.append(
            (has_up, has_down, remote(
                edges.at[side, 0], rims.at[target, groups + 1], edge_send.at[slot + 1],
                edge_recv.at[slot + 1], up, to_lon,
            ))
        )
        rim_copies.append(
            (has_down, has_up, remote(
                edges.at[side, groups - 1], rims.at[target, 0], edge_send.at[slot + 2],
                edge_recv.at[slot + 2], down, to_lon,
            ))
        )

    def run(condition, act):
        if condition is None:
            act()
        else:
            pl.when(condition)(act)

    for sends, _, copy in rim_copies:
        run(sends, copy.start)

    @pl.when(has_up)
    def _():
        to_down.wait_recv()
        for k in range(HALO):
            xt[k, HALO : HALO + cols, :] = turned(top[k])

    @pl.when(has_down)
    def _():
        to_up.wait_recv()
        for k in range(HALO):
            xt[rows + HALO + k, HALO : HALO + cols, :] = turned(bottom[k])

    for _, receives, copy in rim_copies:
        run(receives, copy.wait_recv)

    def spread(step, carry):
        left = rims[0, step].astype(F32)
        right = rims[1, step].astype(F32)
        for k in range(4):
            r = step * 4 + k
            xt[r, 0:HALO, :] = left[k * HALO : (k + 1) * HALO]
            xt[r, HALO + cols : 2 * HALO + cols, :] = right[k * HALO : (k + 1) * HALO]
            for phase in range(6):
                part = xt[r, pl.ds(phase, wide, 4), :]
                xa[pl.ds(r * wide, wide), phase * 128 : (phase + 1) * 128] = part.astype(BF)
        return carry

    low = jnp.where(has_up, 0, 1)
    high = jnp.where(has_down, groups + 2, groups + 1)
    lax.fori_loop(low, high, spread, 0)

    @pl.when(lat == 0)
    def _():
        xa[0 : HALO * wide, :] = jnp.zeros((HALO * wide, xa.shape[1]), BF)

    @pl.when(lat == bands - 1)
    def _():
        xa[(rows + HALO) * wide :, :] = jnp.zeros((HALO * wide, xa.shape[1]), BF)

    bias1 = jnp.concatenate([b1_ref[...], b1_ref[...]], axis=1)

    def conv1(step, carry):
        pair = []
        for side in range(2):
            total = bias1
            for dy in range(3):
                lhs = xa[
                    pl.ds((2 * step + dy) * wide, 2 * wide), side * 256 : side * 256 + 512
                ]
                total = total + dot(lhs, w1[dy])
            pair.append(silu(total))
        for k in range(2):
            row = lat * rows + 2 * step + k - 3
            inside = (row >= 0) & (row < bands * rows)
            where = pl.ds(step * wide, wide)
            a = jnp.where(inside, pair[0][k * wide : (k + 1) * wide], 0.0)
            b = jnp.where(inside, pair[1][k * wide : (k + 1) * wide], 0.0)
            first[k, where, 0:256] = a.astype(BF)
            first[k, where, 256:512] = b.astype(BF)
            first[k, where, 512:768] = pltpu.roll(a, wide - 1, 0).astype(BF)
        return carry

    lax.fori_loop(0, (rows + 6) // 2, conv1, 0)

    half = rows // 2
    weights[0].wait()

    def conv2(step, carry):
        sides = []
        for side in range(2):
            total = b2_ref[...]
            for dy in range(4):
                lhs = first[
                    dy % 2,
                    pl.ds((2 * step + dy // 2) * wide, 2 * wide),
                    side * 256 : side * 256 + 512,
                ]
                total = total + dot(lhs, w2_ref[dy])
            sides.append(silu(total))
        for k in range(2):
            row = lat * half + 2 * step + k - 1
            inside = (row >= 0) & (row < bands * half)
            where = pl.ds(step * tokens, tokens)
            for side in range(2):
                a = jnp.where(inside, sides[side][k * wide : (k + 1) * wide], 0.0)
                second[k, where, side * 256 : side * 256 + 256] = a[:tokens].astype(BF)
                second[k, where, 512 + side * 256 : 768 + side * 256] = pltpu.roll(
                    a, wide - 1, 0
                )[:tokens].astype(BF)
        return carry

    lax.fori_loop(0, (half + 2) // 2, conv2, 0)

    final = rows // 4
    parts = 2
    part = final // parts
    copies = max(1, sectors // final)
    each = max(1, final // sectors)
    width = w3_ref.shape[2]
    long = sectors * tokens
    share = long // copies
    weights[1].wait()

    def go(peer):
        begin = peer // copies * each
        return remote(
            local.at[pl.ds(begin, each)],
            whole.at[:, pl.ds(lon * tokens, tokens)],
            go_send.at[peer], go_recv.at[lon], lat, peer,
        )

    for step in range(parts):
        total = b3_ref[...]
        for dy in range(4):
            begin = (step * part + dy // 2) * tokens
            lhs = second[dy % 2, begin : begin + part * tokens, :]
            total = total + dot(lhs, w3_ref[dy])
        local[step * part : (step + 1) * part] = (
            silu(total).astype(BF).reshape(part, tokens, width)
        )
        for peer in range(sectors):
            if (peer // copies * each) // part == step:
                @pl.when(lon != peer)
                def _():
                    go(peer).start()

    mine_at = lon // copies * each
    whole[:, pl.ds(pl.multiple_of(lon * tokens, tokens), tokens), :] = local[
        pl.ds(mine_at, each)
    ]
    weights[2].wait()
    weights[3].wait()
    for peer in range(sectors):
        @pl.when(lon != peer)
        def _():
            remote(
                local.at[pl.ds(0, each)], whole.at[:, peer * tokens : (peer + 1) * tokens],
                go_send.at[peer], go_recv.at[peer], lat, peer,
            ).wait_recv()

    depth = width // HEADS
    lane = lax.broadcasted_iota(jnp.int32, (1, width), 1)
    scale = jnp.zeros((1, width), F32)
    for h in range(HEADS):
        inside = (lane >= h * depth) & (lane < (h + 1) * depth)
        scale = jnp.where(inside, sharp_ref[h] / jnp.sqrt(F32(depth)), scale)
    block = min(256, share)
    query_at = lax.rem(lon, copies) * share

    def back(i, peer, src_at):
        return remote(
            enc.at[i, pl.ds(src_at, tokens)], landed.at[lon // copies * each + i],
            back_send.at[i, peer], back_recv.at[i, lon], lat, peer,
        )

    for i in range(each):
        feats = whole[i].astype(F32)
        mean = jnp.mean(feats, axis=-1, keepdims=True)
        centred = feats - mean
        variance = jnp.mean(centred * centred, axis=-1, keepdims=True)
        normed = (centred * lax.rsqrt(variance + 1e-05) * gain_ref[...]).astype(BF)
        qs[i] = (dot(normed, wqkv_ref[:, :width]) * scale).astype(BF)
        ks[i] = dot(normed, wqkv_ref[:, width : 2 * width]).astype(BF)
        vs[i] = dot(normed, wqkv_ref[:, 2 * width :]).astype(BF)
        k = ks[i]
        v = vs[i]

        def attend(step, carry):
            at = pl.multiple_of(query_at + step * block, block)
            q = qs[i, pl.ds(at, block), :]
            joined = jnp.zeros((block, width), F32)
            for h in range(HEADS):
                inside = (lane >= h * depth) & (lane < (h + 1) * depth)
                masked = jnp.where(inside, q.astype(F32), 0.0).astype(BF)
                scores = lax.dot_general(
                    masked, k, (((1,), (1,)), ((), ())), preferred_element_type=F32
                )
                raised = jnp.exp(scores - jnp.max(scores, axis=-1, keepdims=True))
                total = jnp.sum(raised, axis=-1, keepdims=True)
                summed = dot(raised.astype(BF), v)
                joined = jnp.where(inside, summed / total, joined)
            mixed = dot(joined.astype(BF), wo_ref[...])
            res = whole[i, pl.ds(at, block), :].astype(F32)
            enc[i, pl.ds(at, block), :] = (res + mixed).astype(BF)
            return carry

        if share == block:
            attend(0, 0)
        else:
            lax.fori_loop(0, share // block, attend, 0)
        for peer in range(sectors):
            @pl.when((lon != peer) & (lax.rem(lon, copies) == peer * copies // sectors))
            def _():
                back(i, peer, peer * tokens).start()

        @pl.when(lax.rem(lon, copies) == lon * copies // sectors)
        def _():
            landed[lon // copies * each + i] = enc[
                i, pl.ds(pl.multiple_of(lon * tokens, tokens), tokens), :
            ]

    for i in range(each):
        for peer in range(sectors):
            @pl.when((lon != peer) & (lon * copies // sectors == peer % copies))
            def _():
                remote(
                    enc.at[i, 0:tokens], landed.at[peer // copies * each + i],
                    back_send.at[i, peer], back_recv.at[i, peer], lat, peer,
                ).wait_recv()
    out_ref[...] = landed[...]

    for sends, copy in ((has_up, to_up), (has_down, to_down)):
        run(sends, copy.wait_send)
    for sends, _, copy in rim_copies:
        run(sends, copy.wait_send)
    for peer in range(sectors):
        @pl.when(lon != peer)
        def _():
            go(peer).wait_send()
    for i in range(each):
        for peer in range(sectors):
            @pl.when((lon != peer) & (lax.rem(lon, copies) == peer * copies // sectors))
            def _():
                back(i, peer, peer * tokens).wait_send()


VM = pl.BlockSpec(memory_space=pltpu.VMEM)
SM = pl.BlockSpec(memory_space=pltpu.SMEM)
HB = pl.BlockSpec(memory_space=pl.ANY)


def on_device(x, taps1, b1, taps2, b2, taps3, b3, gain, wqkv, sharp, wo):
    rows, cin, cols = x.shape
    tokens = cols // 4
    sectors = lax.axis_size("lon")
    width = taps3.shape[3]
    wide = -(-(tokens + 2) // 16) * 16
    final = rows // 4
    each = max(1, final // sectors)
    long = sectors * tokens
    w2 = taps2.reshape(4, -1, width)
    w3 = taps3.reshape(4, -1, width)
    dma = pltpu.SemaphoreType.DMA
    return pl.pallas_call(
        functools.partial(kernel, wide),
        out_shape=jax.ShapeDtypeStruct((final, tokens, width), BF),
        in_specs=[VM, VM, VM, HB, VM, HB, VM, VM, HB, SM, HB],
        out_specs=VM,
        scratch_shapes=[
            pltpu.VMEM(w2.shape, BF),
            pltpu.VMEM(w3.shape, BF),
            pltpu.VMEM(wqkv.shape, BF),
            pltpu.VMEM(wo.shape, BF),
            pltpu.VMEM((3, 512, 256), BF),
            pltpu.VMEM((HALO, cin, cols), BF),
            pltpu.VMEM((HALO, cin, cols), BF),
            pltpu.VMEM((2, rows // 4, 16, 128), BF),
            pltpu.VMEM((2, rows // 4 + 2, 16, 128), BF),
            pltpu.VMEM((rows + 2 * HALO, 4 * wide + 8, 128), F32),
            pltpu.VMEM(((rows + 2 * HALO) * wide, 768), BF),
            pltpu.VMEM((2, (rows + 6) // 2 * wide, 768), BF),
            pltpu.VMEM((2, (rows // 2 + 2) // 2 * tokens, 1024), BF),
            pltpu.VMEM((final, tokens, width), BF),
        ]
        + [pltpu.VMEM((each, long, width), BF)] * 6
        + [
            pltpu.VMEM((final, tokens, width), BF),
            dma((4,)),
            dma((4,)),
            dma((6,)),
            dma((6,)),
            dma((sectors,)),
            dma((sectors,)),
            dma((each, sectors)),
            dma((each, sectors)),
        ],
        compiler_params=pltpu.CompilerParams(
            vmem_limit_bytes=60 * 2**20, collective_id=0, has_side_effects=True
        ),
        name="encoder",
    )(x, taps1, b1[None], w2, b2[None], w3, b3[None], gain[None], wqkv, sharp, wo)


def solution(mesh):
    return jax.shard_map(
        on_device,
        mesh=mesh,
        in_specs=(P("lat", None, "lon"), P(), P(), P(), P(), P(), P(), P(), P(), P(), P()),
        out_specs=P("lat", "lon", None),
        check_vma=False,
    )
```

time: 72.6 us -> 46.7 us (0.64)
  the two profiles are of different devices: /device:TPU:0 before, /device:TPU:17 now
where the time goes in v2:
time: 46.7 us; the launch traced here: 46.5 us
  Pallas kernels  44.9 us (96%)
  local copies, waits for them, and re-layouts  1.67 us (4%)
    pallas_call x1, Pallas kernels, on_device(): pl.pallas_call(functools.partial(kernel, wide), out_shape=jax.ShapeDtypeS...  44.9 us
    unnamed x1, local copies, waits for them, and re-layouts  1.67 us

profile of v2, /device:TPU:17, one launch (start us, length us, event | category | flops | bytes accessed | tf_op | source)
XLA Modules:
  0.0 46.5 jit_solution(4919726211081597931)
XLA Ops:
  0.0 44.9 %encoder.1 = bf16[8,64,256]{2,1,0:T(8,128)(2,1)} custom-call(bf16[32,96,256]{2,1,0:T(8,128)(2,1)} %x_ref.1, bf16[3,3,96,128]{3,2,1,0:T(8,128)(2,1)} %taps_ref.1, f32[1,128]{1,0:T(1,128)} %bitcast.11, bf16[4,512,256]{2,1,0:T(8,128)(2,1)} %bitcast.7, f32[1,256]{1,0:T(1,128)} %bitcast.8, bf16[4,1024,256]{2,1,0:T(8,128)(2,1)} %bitcast.6, f32[1,256]{1,0:T(1,128)} %bitcast.9, ...), custom_call_target="tpu_custom_call" | custom-call | tf_op jit(solution)/shard_map/encoder/pallas_call | solution.py:400
  44.9 1.7 %copy.13 = bf16[8,64,256]{2,1,0:T(8,128)(2,1)} copy(bf16[8,64,256]{2,1,0:T(8,128)(2,1)} %encoder.1) | data formatting | bytes 524288

commit v3 on v2

--- a/solution.py
+++ b/solution.py
@@ -194,58 +194,91 @@
         xa[(rows + HALO) * wide :, :] = jnp.zeros((HALO * wide, xa.shape[1]), BF)
 
     bias1 = jnp.concatenate([b1_ref[...], b1_ref[...]], axis=1)
-
-    def conv1(step, carry):
+    kernel1 = w1[...].reshape(1536, 256)
+
+    def conv1(step, steps):
+        count = 2 * steps
         pair = []
         for side in range(2):
-            total = bias1
-            for dy in range(3):
-                lhs = xa[
-                    pl.ds((2 * step + dy) * wide, 2 * wide), side * 256 : side * 256 + 512
-                ]
-                total = total + dot(lhs, w1[dy])
-            pair.append(silu(total))
-        for k in range(2):
-            row = lat * rows + 2 * step + k - 3
-            inside = (row >= 0) & (row < bands * rows)
-            where = pl.ds(step * wide, wide)
-            a = jnp.where(inside, pair[0][k * wide : (k + 1) * wide], 0.0)
-            b = jnp.where(inside, pair[1][k * wide : (k + 1) * wide], 0.0)
-            first[k, where, 0:256] = a.astype(BF)
-            first[k, where, 256:512] = b.astype(BF)
-            first[k, where, 512:768] = pltpu.roll(a, wide - 1, 0).astype(BF)
+            lhs = jnp.concatenate(
+                [
+                    xa[pl.ds((2 * step + dy) * wide, count * wide), side * 256 : side * 256 + 512]
+                    for dy in range(3)
+                ],
+                axis=1,
+            )
+            pair.append(silu(dot(lhs, kernel1) + bias1))
+        for k in range(count):
+            where = pl.ds((step + k // 2) * wide, wide)
+            one = pair[0][k * wide : (k + 1) * wide]
+            two = pair[1][k * wide : (k + 1) * wide]
+            first[k % 2, where, 0:256] = one.astype(BF)
+            first[k % 2, where, 256:512] = two.astype(BF)
+            first[k % 2, where, 512:768] = pltpu.roll(one, wide - 1, 0).astype(BF)
+
+    steps1 = (rows + 6) // 2
+
+    def conv1_body(step, carry):
+        conv1(2 * step, 2)
         return carry
 
-    lax.fori_loop(0, (rows + 6) // 2, conv1, 0)
+    lax.fori_loop(0, steps1 // 2, conv1_body, 0)
+    if steps1 % 2:
+        conv1(steps1 - 1, 1)
+
+    @pl.when(lat == 0)
+    def _():
+        for r in range(3):
+            begin = r // 2 * wide
+            first[r % 2, begin : begin + wide, :] = jnp.zeros((wide, 768), BF)
+
+    @pl.when(lat == bands - 1)
+    def _():
+        for r in range(rows + 3, rows + 6):
+            begin = r // 2 * wide
+            first[r % 2, begin : begin + wide, :] = jnp.zeros((wide, 768), BF)
 
     half = rows // 2
     weights[0].wait()
-
-    def conv2(step, carry):
-        sides = []
+    kernel2 = w2_ref[...].reshape(2048, 256)
+    steps2 = (half + 2) // 2
+    group = 3 if steps2 % 3 == 0 else 1
+    count2 = 2 * group
+
+    def conv2(chunk, carry):
+        step = chunk * group
         for side in range(2):
-            total = b2_ref[...]
-            for dy in range(4):
-                lhs = first[
-                    dy % 2,
-                    pl.ds((2 * step + dy // 2) * wide, 2 * wide),
-                    side * 256 : side * 256 + 512,
-                ]
-                total = total + dot(lhs, w2_ref[dy])
-            sides.append(silu(total))
-        for k in range(2):
-            row = lat * half + 2 * step + k - 1
-            inside = (row >= 0) & (row < bands * half)
-            where = pl.ds(step * tokens, tokens)
-            for side in range(2):
-                a = jnp.where(inside, sides[side][k * wide : (k + 1) * wide], 0.0)
-                second[k, where, side * 256 : side * 256 + 256] = a[:tokens].astype(BF)
-                second[k, where, 512 + side * 256 : 768 + side * 256] = pltpu.roll(
+            lhs = jnp.concatenate(
+                [
+                    first[
+                        dy % 2,
+                        pl.ds((2 * step + dy // 2) * wide, count2 * wide),
+                        side * 256 : side * 256 + 512,
+                    ]
+                    for dy in range(4)
+                ],
+                axis=1,
+            )
+            result = silu(dot(lhs, kernel2) + b2_ref[...])
+            for k in range(count2):
+                where = pl.ds((step + k // 2) * tokens, tokens)
+                a = result[k * wide : (k + 1) * wide]
+                second[k % 2, where, side * 256 : side * 256 + 256] = a[:tokens].astype(BF)
+                second[k % 2, where, 512 + side * 256 : 768 + side * 256] = pltpu.roll(
                     a, wide - 1, 0
                 )[:tokens].astype(BF)
         return carry
 
-    lax.fori_loop(0, (half + 2) // 2, conv2, 0)
+    lax.fori_loop(0, steps2 // group, conv2, 0)
+
+    @pl.when(lat == 0)
+    def _():
+        second[0, 0:tokens, :] = jnp.zeros((tokens, 1024), BF)
+
+    @pl.when(lat == bands - 1)
+    def _():
+        begin = (half + 1) // 2 * tokens
+        second[1, begin : begin + tokens, :] = jnp.zeros((tokens, 1024), BF)
 
     final = rows // 4
     parts = 2

time: 46.7 us -> 43.8 us (0.938)
  Pallas kernels: 44.9 us -> 42 us
    pallas_call x1, Pallas kernels: 44.9 us -> 42 us  [on_device(): pl.pallas_call(functools.partial(kernel, wide), out_shape=jax.ShapeDtypeS...]
where the time goes in v3:
time: 43.8 us; the launch traced here: 43.6 us
  Pallas kernels  42 us (96%)
  local copies, waits for them, and re-layouts  1.67 us (4%)
    pallas_call x1, Pallas kernels, on_device(): pl.pallas_call(functools.partial(kernel, wide), out_shape=jax.ShapeDtypeS...  42 us
    unnamed x1, local copies, waits for them, and re-layouts  1.67 us

profile of v3, /device:TPU:17, one launch (start us, length us, event | category | flops | bytes accessed | tf_op | source)
XLA Modules:
  0.0 43.6 jit_solution(6794528666809088131)
XLA Ops:
  0.0 42.0 %encoder.1 = bf16[8,64,256]{2,1,0:T(8,128)(2,1)} custom-call(bf16[32,96,256]{2,1,0:T(8,128)(2,1)} %x_ref.1, bf16[3,3,96,128]{3,2,1,0:T(8,128)(2,1)} %taps_ref.1, f32[1,128]{1,0:T(1,128)} %bitcast.11, bf16[4,512,256]{2,1,0:T(8,128)(2,1)} %bitcast.7, f32[1,256]{1,0:T(1,128)} %bitcast.8, bf16[4,1024,256]{2,1,0:T(8,128)(2,1)} %bitcast.6, f32[1,256]{1,0:T(1,128)} %bitcast.9, ...), custom_call_target="tpu_custom_call" | custom-call | tf_op jit(solution)/shard_map/encoder/pallas_call | solution.py:433
  42.0 1.7 %copy.13 = bf16[8,64,256]{2,1,0:T(8,128)(2,1)} copy(bf16[8,64,256]{2,1,0:T(8,128)(2,1)} %encoder.1) | data formatting | bytes 524288
